TPU v7x, 512 devices: a whole 4x8x8 slice. The times are simulated.
512 devices in a mesh: blk: 64 (over x, y, z_hi), edge: 8 (over z_lo, core).
Axes of the slice: x: 4, y: 8, z: 8 (z_hi: 2, z_lo: 4; z = z_hi * 4 + z_lo), core: 2. Of those that a mesh axis runs over, the one named last changes fastest.
Arguments:
- node_feat: bfloat16 [8192, 128], P(('blk', 'edge')), may hold values from -6 to 6
- coords: bfloat16 [3, 8192], P(None, ('blk', 'edge')), may hold values from -4 to 4
- pair_table: int32 [3, 64], replicated, may hold values from 0 to 63, as said below
- w_tgt: bfloat16 [128, 128], replicated, may hold values from -0.375 to 0.375
- w_src: bfloat16 [128, 128], replicated, may hold values from -0.375 to 0.375
- w_dist: float32 [128], replicated, may hold values from -0.8 to 0.8
- edge_bias: float32 [128], replicated, may hold values from -2 to 2
- w_edge: bfloat16 [128, 128], replicated, may hold values from -0.5 to 0.5
- w_gate: float32 [128], replicated, may hold values from -1.5 to 1.5
- w_coord: bfloat16 [128, 128], replicated, may hold values from -0.5 to 0.5
- w_weight: float32 [128], replicated, may hold values from -5 to 5
- w_node_in: bfloat16 [256, 128], replicated, may hold values from -0.375 to 0.375
- w_node_out: bfloat16 [128, 128], replicated, may hold values from -0.5 to 0.5
Outputs:
- new_feat: bfloat16 [8192, 128], P(('blk', 'edge'))
- new_coords: float32 [3, 8192], P(None, ('blk', 'edge'))
Inputs may be any that keep to these rules, and one draw needn't show every extreme that they name: Each row pairs the 64 blocks: pair_table[r, b] = c exactly when pair_table[r, c] = b, and c is never b; no block meets the same partner in two rows.
All inputs are finite; a program needn't handle non-finite values.
Results may differ from a plain program's by a relative error of at most 0.0027.
Values may be sent and summed in bfloat16 or wider, within the bound.
A program may use at most 128 MiB of HBM per device.

v0:
```python
import math

import jax
import jax.numpy as jnp
from jax import lax
from jax.sharding import PartitionSpec as P


def rows_first(arrays, axis, dims):
    turned = [jnp.moveaxis(a, dim, 0) for a, dim in zip(arrays, dims)]
    widths = [t[0].size for t in turned]
    both = jnp.concatenate([t.reshape(-1, w) for t, w in zip(turned, widths)], axis=1)
    filled = lax.all_gather(both, axis, axis=0, tiled=True)
    blocks = jnp.split(filled, [sum(widths[:k]) for k in range(1, len(widths))], axis=1)
    return tuple(
        (
            jnp.moveaxis(b.reshape(-1, *t.shape[1:]), 0, dim)
            for b, t, dim in zip(blocks, turned, dims)
        )
    )


def in_one_piece(arrays, axis, dim, along):
    widths = [math.prod(a.shape[along:]) for a in arrays]
    both = jnp.concatenate(
        [a.reshape(*a.shape[:along], w) for a, w in zip(arrays, widths)], axis=along
    )
    filled = lax.all_gather(both, axis, axis=dim, tiled=True)
    blocks = jnp.split(filled, [sum(widths[:k]) for k in range(1, len(widths))], axis=along)
    return tuple(
        (b.reshape(*filled.shape[:along], *a.shape[along:]) for a, b in zip(arrays, blocks))
    )


def split_up(shard, dim, peers):
    shape = shard.shape
    blocks = shard.reshape(*shape[:dim], peers, shape[dim] // peers, *shape[dim + 1 :])
    return jnp.moveaxis(blocks, dim, 0)


def sent_and_summed(shard, axis, dim):
    peers = lax.axis_size(axis)
    blocks = lax.all_to_all(split_up(shard, dim, peers), axis, 0, 0, tiled=True)
    return jnp.sum(blocks, axis=0)


def edge_terms(
    tgt_proj,
    tgt_place,
    src_feat,
    src_place,
    keep_mask,
    w_src,
    w_dist,
    edge_bias,
    w_edge,
    w_gate,
    w_coord,
    w_weight,
):
    src_proj = jnp.dot(src_feat, w_src, preferred_element_type=jnp.float32)
    offset = tgt_place.astype(jnp.float32)[:, :, None] - src_place.astype(jnp.float32)[:, None, :]
    radial = jnp.sum(offset * offset, axis=0)
    targets = radial.shape[0]
    sources = radial.shape[1]
    pre_act = tgt_proj[:, None, :] + src_proj[None, :, :] + radial[:, :, None] * w_dist + edge_bias
    hidden = jax.nn.silu(pre_act).astype(jnp.bfloat16).reshape(targets * sources, -1)
    message = jax.nn.silu(jnp.dot(hidden, w_edge, preferred_element_type=jnp.float32))
    edge_gate = (
        jax.nn.sigmoid(jnp.sum(message * w_gate, axis=1)).reshape(targets, sources) * keep_mask
    )
    lifted = jax.nn.silu(
        jnp.dot(message.astype(jnp.bfloat16), w_coord, preferred_element_type=jnp.float32)
    )
    weight = jnp.sum(lifted * w_weight, axis=1).reshape(targets, sources) * keep_mask
    message_sum = jnp.sum(message.reshape(targets, sources, -1) * edge_gate[:, :, None], axis=1)
    unit_dir = offset / (jnp.sqrt(radial) + 1.0)
    coord_sum = jnp.sum(unit_dir * weight[None], axis=2)
    return (message_sum, coord_sum)


def shards(
    node_feat,
    coords,
    pair_table,
    w_tgt,
    w_src,
    w_dist,
    edge_bias,
    w_edge,
    w_gate,
    w_coord,
    w_weight,
    w_node_in,
    w_node_out,
):
    row_count = node_feat.shape[0]
    feat_width = node_feat.shape[1]
    edge_parts = lax.axis_size("edge")
    block_index = lax.axis_index("blk")
    edge_index = lax.axis_index("edge")
    rounds = pair_table.shape[0]
    block_size = row_count * edge_parts
    mean_scale = 1.0 / ((rounds + 1) * block_size - 1)
    weights = (w_src, w_dist, edge_bias, w_edge, w_gate, w_coord, w_weight)
    block_feat, block_place = rows_first((node_feat, coords), "edge", (0, 1))
    partners = lax.dynamic_index_in_dim(pair_table, block_index, 1, keepdims=False)
    tgt_proj = jnp.dot(block_feat, w_tgt, preferred_element_type=jnp.float32)
    target_ids = jnp.arange(block_size, dtype=jnp.int32)
    source_ids = edge_index * row_count + jnp.arange(row_count, dtype=jnp.int32)
    self_keep = (target_ids[:, None] != source_ids[None, :]).astype(jnp.float32)
    all_keep = jnp.ones((block_size, row_count), jnp.float32)
    term_list = [edge_terms(tgt_proj, block_place, node_feat, coords, self_keep, *weights)]
    far_feat, far_place = in_one_piece((node_feat[None], coords[None]), "blk", 0, 1)
    for round_step in range(rounds):
        partner = partners[round_step]
        src_feat = lax.dynamic_index_in_dim(far_feat, partner, 0, keepdims=False)
        src_place = lax.dynamic_index_in_dim(far_place, partner, 0, keepdims=False)
        term_list.append(edge_terms(tgt_proj, block_place, src_feat, src_place, all_keep, *weights))
    message_total = jnp.zeros((row_count, feat_width), jnp.float32)
    coord_total = jnp.zeros((3, row_count), jnp.float32)
    for message_sum, coord_sum in term_list:
        message_part, coord_part = (
            sent_and_summed(message_sum, "edge", 0),
            sent_and_summed(coord_sum, "edge", 1),
        )
        message_total = message_total + message_part
        coord_total = coord_total + coord_part
    message_mean = (message_total * mean_scale).astype(jnp.bfloat16)
    node_pre = jnp.dot(
        node_feat, w_node_in[:feat_width], preferred_element_type=jnp.float32
    ) + jnp.dot(message_mean, w_node_in[feat_width:], preferred_element_type=jnp.float32)
    node_hidden = jax.nn.silu(node_pre).astype(jnp.bfloat16)
    new_feat = (
        node_feat.astype(jnp.float32)
        + jnp.dot(node_hidden, w_node_out, preferred_element_type=jnp.float32)
    ).astype(jnp.bfloat16)
    new_coords = coords.astype(jnp.float32) + coord_total * mean_scale
    return (new_feat, new_coords)


def solution(mesh):
    placed = (
        P(("blk", "edge"), None),
        P(None, ("blk", "edge")),
        P(),
        P(),
        P(),
        P(),
        P(),
        P(),
        P(),
        P(),
        P(),
        P(),
        P(),
    )
    return jax.shard_map(
        shards,
        mesh=mesh,
        in_specs=placed,
        out_specs=(P(("blk", "edge"), None), P(None, ("blk", "edge"))),
        check_vma=False,
    )
```

profile of v0, /device:TPU:1, one launch (start us, length us, event | category | flops | bytes accessed | tf_op | source)
XLA Modules:
  0.0 346.6 jit_solution(3064935569369761217)
XLA Ops:
  0.7 0.7 copy-done.11
  6.8 203.4 %all-gather = bf16[64,1,2096]{2,1,0:T(2,128)(2,1)S(1)} all-gather(bf16[1,1,2096]{2,1,0:T(2,128)(2,1)S(1)} %maximum_bitcast_fusion), channel_id=1, replica_groups=mesh['blk'=64,'edge'=8] {'blk'}, dimensions={0}, use_global_device_ids=true | all-gather | bytes 272480 | tf_op jit(solution)/shard_map/all_gather | solution.py:28
  210.3 0.7 copy-done.3
  213.7 42.6 %all_gather.6 = bf16[128,131]{1,0:T(8,128)(2,1)S(1)} all-gather(bf16[16,131]{1,0:T(8,128)(2,1)S(1)} %pad_maximum_fusion), channel_id=1, replica_groups=mesh['blk'=64,'edge'=8] {'edge'}, dimensions={0}, use_global_device_ids=true | all-gather | bytes 37728 | tf_op jit(solution)/shard_map/all_gather | solution.py:13
  257.0 0.7 copy-done.7
  258.0 1.3 broadcast_add_fusion
  259.9 1.6 multiply_convert_fusion.3
  263.2 1.3 fusion.65
  265.8 1.9 multiply_convert_fusion
  269.4 1.2 multiply_reduce_fusion.9
  270.6 1.0 copy-done.1
  273.4 3.9 %all-to-all-start.6 = ((f32[8,3,16]{2,1,0:T(4,128)}), f32[8,3,16]{2,1,0:T(4,128)S(1)}, u32[]{:S(2)}, u32[]{:S(2)}) async-start(f32[8,3,16]{2,1,0:T(4,128)} %copy.101), calls=%async_computation.6 | async-start | bytes 32768 | tf_op jit(solution)/shard_map/all_to_all | solution.py:43
  277.3 1.1 multiply_reduce_fusion.8
  279.2 3.0 all-to-all-done.6
  282.2 4.0 %all-to-all-start.7 = ((f32[8,3,16]{2,1,0:T(4,128)}), f32[8,3,16]{2,1,0:T(4,128)S(1)}, u32[]{:S(2)}, u32[]{:S(2)}) async-start(f32[8,3,16]{2,1,0:T(4,128)} %copy.105), calls=%async_computation.7 | async-start | bytes 32768 | tf_op jit(solution)/shard_map/all_to_all | solution.py:43
  286.1 1.1 multiply_reduce_fusion.10
  287.9 3.2 all-to-all-done.7
  291.1 3.9 %all-to-all-start.4 = ((f32[8,3,16]{2,1,0:T(4,128)}), f32[8,3,16]{2,1,0:T(4,128)S(1)}, u32[]{:S(2)}, u32[]{:S(2)}) async-start(f32[8,3,16]{2,1,0:T(4,128)} %copy.93), calls=%async_computation.4 | async-start | bytes 32768 | tf_op jit(solution)/shard_map/all_to_all | solution.py:43
  295.8 4.2 %all-to-all-done.4 = f32[8,3,16]{2,1,0:T(4,128)S(1)} async-done(((f32[8,3,16]{2,1,0:T(4,128)}), f32[8,3,16]{2,1,0:T(4,128)S(1)}, u32[]{:S(2)}, u32[]{:S(2)}) %all-to-all-start.4) | async-done | bytes 1568 | tf_op jit(solution)/shard_map/all_to_all | solution.py:43
  300.0 4.0 %all-to-all-start.5 = ((f32[8,3,16]{2,1,0:T(4,128)}), f32[8,3,16]{2,1,0:T(4,128)S(1)}, u32[]{:S(2)}, u32[]{:S(2)}) async-start(f32[8,3,16]{2,1,0:T(4,128)} %copy.97), calls=%async_computation.5 | async-start | bytes 32768 | tf_op jit(solution)/shard_map/all_to_all | solution.py:43
  303.9 1.1 multiply_reduce_fusion.6
  305.0 3.9 %all-to-all-done.5 = f32[8,3,16]{2,1,0:T(4,128)S(1)} async-done(((f32[8,3,16]{2,1,0:T(4,128)}), f32[8,3,16]{2,1,0:T(4,128)S(1)}, u32[]{:S(2)}, u32[]{:S(2)}) %all-to-all-start.5) | async-done | bytes 1568 | tf_op jit(solution)/shard_map/all_to_all | solution.py:43
  308.9 4.0 %all-to-all-start.1 = ((f32[8,16,128]{2,1,0:T(8,128)}), f32[8,16,128]{2,1,0:T(8,128)S(1)}, u32[]{:S(2)}, u32[]{:S(2)}) async-start(f32[8,16,128]{2,1,0:T(8,128)} %bitcast.11), calls=%async_computation.1 | async-start | bytes 131072 | tf_op jit(solution)/shard_map/all_to_all | solution.py:43
  313.0 5.0 %all-to-all-done.1 = f32[8,16,128]{2,1,0:T(8,128)S(1)} async-done(((f32[8,16,128]{2,1,0:T(8,128)}), f32[8,16,128]{2,1,0:T(8,128)S(1)}, u32[]{:S(2)}, u32[]{:S(2)}) %all-to-all-start.1) | async-done | bytes 65568 | tf_op jit(solution)/shard_map/all_to_all | solution.py:43
  318.0 4.1 %all-to-all-start = ((f32[8,16,128]{2,1,0:T(8,128)}), f32[8,16,128]{2,1,0:T(8,128)S(1)}, u32[]{:S(2)}, u32[]{:S(2)}) async-start(f32[8,16,128]{2,1,0:T(8,128)} %bitcast.4), calls=%async_computation | async-start | bytes 131072 | tf_op jit(solution)/shard_map/all_to_all | solution.py:43
  322.1 1.1 multiply_reduce_fusion.4
  323.1 4.1 %all-to-all-done = f32[8,16,128]{2,1,0:T(8,128)S(1)} async-done(((f32[8,16,128]{2,1,0:T(8,128)}), f32[8,16,128]{2,1,0:T(8,128)S(1)}, u32[]{:S(2)}, u32[]{:S(2)}) %all-to-all-start) | async-done | bytes 65568 | tf_op jit(solution)/shard_map/all_to_all | solution.py:43
  327.2 4.2 %all-to-all-start.2 = ((f32[8,16,128]{2,1,0:T(8,128)}), f32[8,16,128]{2,1,0:T(8,128)S(1)}, u32[]{:S(2)}, u32[]{:S(2)}) async-start(f32[8,16,128]{2,1,0:T(8,128)} %bitcast.16), calls=%async_computation.2 | async-start | bytes 131072 | tf_op jit(solution)/shard_map/all_to_all | solution.py:43
  331.6 4.9 %all-to-all-done.2 = f32[8,16,128]{2,1,0:T(8,128)S(1)} async-done(((f32[8,16,128]{2,1,0:T(8,128)}), f32[8,16,128]{2,1,0:T(8,128)S(1)}, u32[]{:S(2)}, u32[]{:S(2)}) %all-to-all-start.2) | async-done | bytes 65568 | tf_op jit(solution)/shard_map/all_to_all | solution.py:43
  336.5 4.1 %all-to-all-start.3 = ((f32[8,16,128]{2,1,0:T(8,128)}), f32[8,16,128]{2,1,0:T(8,128)S(1)}, u32[]{:S(2)}, u32[]{:S(2)}) async-start(f32[8,16,128]{2,1,0:T(8,128)} %bitcast.21), calls=%async_computation.3 | async-start | bytes 131072 | tf_op jit(solution)/shard_map/all_to_all | solution.py:43
  341.3 4.5 %all-to-all-done.3 = f32[8,16,128]{2,1,0:T(8,128)S(1)} async-done(((f32[8,16,128]{2,1,0:T(8,128)}), f32[8,16,128]{2,1,0:T(8,128)S(1)}, u32[]{:S(2)}, u32[]{:S(2)}) %all-to-all-start.3) | async-done | bytes 65568 | tf_op jit(solution)/shard_map/all_to_all | solution.py:43
  345.8 0.9 fusion
  (104 shorter events, 13.3 us)
Async XLA Ops:
  0.6 260.9 %copy-start = (bf16[128,128]{1,0:T(8,128)(2,1)S(1)}, bf16[128,128]{1,0:T(8,128)(2,1)}, u32[]{:S(2)}) copy-start(bf16[128,128]{1,0:T(8,128)(2,1)} %param.20) | copy-start | bytes 98308
  0.7 0.7 copy-start.11
  4.7 1.3 copy-start.4
  6.0 0.7 copy-start.8
  210.3 0.8 copy-start.3
  256.9 0.8 copy-start.7
  259.3 0.7 copy-start.9
  259.3 0.7 copy-start.10
  261.6 0.8 copy-start.12
  261.6 0.8 copy-start.14
  268.7 0.7 copy-start.13
  270.6 1.0 copy-start.1
  273.4 8.8 %all-to-all-start.6 = ((f32[8,3,16]{2,1,0:T(4,128)}), f32[8,3,16]{2,1,0:T(4,128)S(1)}, u32[]{:S(2)}, u32[]{:S(2)}) async-start(f32[8,3,16]{2,1,0:T(4,128)} %copy.101), calls=%async_computation.6 | async-start | bytes 32768 | tf_op jit(solution)/shard_map/all_to_all | solution.py:43
  278.4 25.5 %copy-start.2 = (f32[2048,128]{1,0:T(8,128)S(1)}, f32[2048,128]{1,0:T(8,128)}, u32[]{:S(2)}) copy-start(f32[2048,128]{1,0:T(8,128)} %copy-done.1) | copy-start | bytes 3145732
  282.2 8.9 %all-to-all-start.7 = ((f32[8,3,16]{2,1,0:T(4,128)}), f32[8,3,16]{2,1,0:T(4,128)S(1)}, u32[]{:S(2)}, u32[]{:S(2)}) async-start(f32[8,3,16]{2,1,0:T(4,128)} %copy.105), calls=%async_computation.7 | async-start | bytes 32768 | tf_op jit(solution)/shard_map/all_to_all | solution.py:43
  291.1 8.9 %all-to-all-start.4 = ((f32[8,3,16]{2,1,0:T(4,128)}), f32[8,3,16]{2,1,0:T(4,128)S(1)}, u32[]{:S(2)}, u32[]{:S(2)}) async-start(f32[8,3,16]{2,1,0:T(4,128)} %copy.93), calls=%async_computation.4 | async-start | bytes 32768 | tf_op jit(solution)/shard_map/all_to_all | solution.py:43
  300.0 8.9 %all-to-all-start.5 = ((f32[8,3,16]{2,1,0:T(4,128)}), f32[8,3,16]{2,1,0:T(4,128)S(1)}, u32[]{:S(2)}, u32[]{:S(2)}) async-start(f32[8,3,16]{2,1,0:T(4,128)} %copy.97), calls=%async_computation.5 | async-start | bytes 32768 | tf_op jit(solution)/shard_map/all_to_all | solution.py:43
  308.9 9.1 %all-to-all-start.1 = ((f32[8,16,128]{2,1,0:T(8,128)}), f32[8,16,128]{2,1,0:T(8,128)S(1)}, u32[]{:S(2)}, u32[]{:S(2)}) async-start(f32[8,16,128]{2,1,0:T(8,128)} %bitcast.11), calls=%async_computation.1 | async-start | bytes 131072 | tf_op jit(solution)/shard_map/all_to_all | solution.py:43
  318.0 9.2 %all-to-all-start = ((f32[8,16,128]{2,1,0:T(8,128)}), f32[8,16,128]{2,1,0:T(8,128)S(1)}, u32[]{:S(2)}, u32[]{:S(2)}) async-start(f32[8,16,128]{2,1,0:T(8,128)} %bitcast.4), calls=%async_computation | async-start | bytes 131072 | tf_op jit(solution)/shard_map/all_to_all | solution.py:43
  327.2 4.2 %copy-start.5 = (bf16[256,128]{1,0:T(8,128)(2,1)S(1)}, bf16[256,128]{1,0:T(8,128)(2,1)}, u32[]{:S(2)}) copy-start(bf16[256,128]{1,0:T(8,128)(2,1)} %param.24) | copy-start | bytes 196612
  327.2 9.3 %all-to-all-start.2 = ((f32[8,16,128]{2,1,0:T(8,128)}), f32[8,16,128]{2,1,0:T(8,128)S(1)}, u32[]{:S(2)}, u32[]{:S(2)}) async-start(f32[8,16,128]{2,1,0:T(8,128)} %bitcast.16), calls=%async_computation.2 | async-start | bytes 131072 | tf_op jit(solution)/shard_map/all_to_all | solution.py:43
  336.5 9.2 %all-to-all-start.3 = ((f32[8,16,128]{2,1,0:T(8,128)}), f32[8,16,128]{2,1,0:T(8,128)S(1)}, u32[]{:S(2)}, u32[]{:S(2)}) async-start(f32[8,16,128]{2,1,0:T(8,128)} %bitcast.21), calls=%async_computation.3 | async-start | bytes 131072 | tf_op jit(solution)/shard_map/all_to_all | solution.py:43
  341.3 4.5 %copy-start.6 = (bf16[128,128]{1,0:T(8,128)(2,1)S(1)}, bf16[128,128]{1,0:T(8,128)(2,1)}, u32[]{:S(2)}) copy-start(bf16[128,128]{1,0:T(8,128)(2,1)} %param.25) | copy-start | bytes 98308
where the time goes:
time: 348 us; the launch traced here: 347 us
  blocking collectives  246 us (71%)
  waiting for transfers between devices  32.7 us (9%)
  starting transfers between devices  32.1 us (9%)
  local copies, waits for them, and re-layouts  11.1 us (3%)
  other arithmetic  10.4 us (3%)
  matrix products  7.39 us (2%)
  between operations  7.01 us (2%)
    all_gather x1, blocking collectives, in_one_piece(): filled = lax.all_gather(both, axis, axis=dim, tiled=True)  203 us
    all_gather x1, blocking collectives, rows_first(): filled = lax.all_gather(both, axis, axis=0, tiled=True)  42.6 us
    all_to_all x8, waiting for transfers between devices, sent_and_summed(): blocks = lax.all_to_all(split_up(shard, dim, peers), axis, 0, 0, tiled=True)  32.7 us
    all_to_all x8, starting transfers between devices, sent_and_summed(): blocks = lax.all_to_all(split_up(shard, dim, peers), axis, 0, 0, tiled=True)  32.1 us
  transfers between devices with their start and end apart: 8, of which 8 were waited for; matrix products, arithmetic and copies ran while one was open for 2% of the time, Pallas kernels for 0%

commit v1 on v0

v1 whole, which is shorter than its diff:
```python
import functools

import jax
import jax.numpy as jnp
from jax import lax
from jax.experimental import pallas as pl
from jax.experimental.pallas import tpu as pltpu
from jax.sharding import PartitionSpec as P

MESH = pl.DeviceIdType.MESH
F32 = jnp.float32
BF16 = jnp.bfloat16

NX, NY, NZ = 4, 8, 8
RING = {4: (2, 1, 3, 0), 8: (4, 3, 5, 2, 6, 1, 7, 0)}
PLANE = [(dx, dy) for dx in RING[NX] for dy in RING[NY] if dx or dy]
COLUMN = [(dz, dc) for dz in RING[NZ] for dc in (1, 0) if dz or dc]
EDGE = (4, 3, 5, 2, 6, 1, 7)
ROWS = 16
TERMS = 16


def iota(shape, dim):
    return lax.broadcasted_iota(jnp.int32, shape, dim)


def dot(a, b, dims=((1,), (0,))):
    return lax.dot_general(a, b, (dims, ((), ())), preferred_element_type=F32)


def split2(a):
    high = a.astype(BF16)
    return high, (a - high.astype(F32)).astype(BF16)


def half_silu(h):
    return h + h * jnp.tanh(h)


def source_rows(places, count):
    slots = places.shape[0]
    lane = iota((128, count), 0)
    node = lax.rem(iota((128, count), 1), 16)
    mine = (iota((slots, count), 1) // 16) == iota((slots, count), 0)
    low = places.astype(BF16)
    rows = []
    for k in range(3):
        spread = dot(low, (lane == node + 16 * k).astype(BF16))
        rows.append(jnp.sum(jnp.where(mine, spread, 0.0), axis=0, keepdims=True))
    return rows


def edge_sums(lhs_ref, base, count, places, own, target_cols, wide_ref, w_edge2, w_coord2, gate_row, weight_row):
    rows = source_rows(places, count)
    norm = rows[0] * rows[0] + rows[1] * rows[1] + rows[2] * rows[2]
    norm_high, norm_mid = split2(norm)
    norm_low = (norm - norm_high.astype(F32) - norm_mid.astype(F32)).astype(F32)
    one = jnp.ones((1, count), F32)
    nh, nm = norm_high.astype(F32), norm_mid.astype(F32)
    terms = rows + rows + [nh, nm, nh, one, one, norm_low]
    terms = jnp.concatenate(terms + [jnp.zeros((TERMS - len(terms), count), F32)], axis=0).astype(BF16)
    place_term = (iota((TERMS, 128), 0) == iota((TERMS, 128), 1)).astype(BF16)
    lhs_ref[pl.ds(base, count), 128:256] = dot(terms, place_term, ((0,), (0,))).astype(BF16)
    lhs = lhs_ref[pl.ds(base, count), :]

    offsets = [target_cols[k][:, :1] - rows[k] for k in range(3)]
    radial = offsets[0] * offsets[0] + offsets[1] * offsets[1] + offsets[2] * offsets[2]
    scale = 1.0 / (jnp.sqrt(radial) + 1.0)

    row16, col16 = iota((16, 256), 0), iota((16, 256), 1)
    message_sum = jnp.zeros((16, 256), F32)
    weights = jnp.zeros((16, count), F32)
    for pair in range(8):
        half = dot(lhs, wide_ref[pair]).astype(BF16)
        hidden = half_silu(half)
        message = half_silu(dot(hidden, w_edge2).astype(BF16))
        lifted = half_silu(dot(message, w_coord2).astype(BF16))
        here = row16 == 2 * pair + col16 // 128
        pick = lambda pieces: jnp.concatenate([jnp.where(here, p, 0.0) for p in pieces], axis=0).astype(BF16)
        logit = dot(pick(gate_row), message, ((1,), (1,)))
        gate = 0.5 + 0.5 * jnp.tanh(logit[:16] + logit[16:])
        if own is not None:
            gate = gate * own
        message_sum = message_sum + jnp.where(here, dot(gate.astype(BF16), message), 0.0)
        weight = dot(pick(weight_row), lifted, ((1,), (1,)))
        weights = weights + (weight[:16] + weight[16:])
    if own is not None:
        weights = weights * own
    weights = weights * scale
    coord_sum = [jnp.sum(offsets[k] * weights, axis=1, keepdims=True) for k in range(3)]
    return message_sum[:, :128] + message_sum[:, 128:], coord_sum


def layer(
    feat_hbm, place_hbm, table_hbm, w_tgt_hbm, w_src_hbm, w_dist_hbm, bias_hbm, w_edge_hbm, w_gate_hbm,
    w_coord_hbm, w_weight_hbm, w_in_hbm, w_out_hbm,
    feat_out, place_out,
    feat, place, table, w_tgt, w_src, w_dist, bias, w_edge, w_gate, w_coord, w_weight, w_in, w_out,
    place_row, near_feat, near_place, plane_feat, plane_place, picked_feat, picked_place,
    column_feat, column_place, lhs, place_list, wide, edge_wide, coord_wide,
    load_sem, send_sem, recv_sem,
):
    blk, edge = lax.axis_index("blk"), lax.axis_index("edge")
    x, y, z_hi = blk // 16, (blk // 2) % 8, blk % 2
    core = edge % 2
    z = z_hi * 4 + edge // 2
    here = x * 8 + y
    spot = z * 2 + core

    plane = [{"blk": (lax.rem(x + dx, NX) * NY + lax.rem(y + dy, NY)) * 2 + z_hi} for dx, dy in PLANE]
    column = []
    for dz, dc in COLUMN:
        z_to = lax.rem(z + dz, NZ)
        column.append(({"blk": here * 2 + z_to // 4, "edge": (z_to % 4) * 2 + lax.rem(core + dc, 2)}, z_to // 4))
    near = [{"edge": lax.rem(edge + step, 8)} for step in EDGE]

    barrier = pltpu.get_barrier_semaphore()
    for peer in plane + [c[0] for c in column]:
        pl.semaphore_signal(barrier, inc=1, device_id=peer, device_id_type=MESH)
    loads = [
        pltpu.make_async_copy(a, b, load_sem.at[k])
        for k, (a, b) in enumerate(
            [
                (feat_hbm, feat), (place_hbm, place), (table_hbm, table), (w_tgt_hbm, w_tgt), (w_src_hbm, w_src),
                (w_dist_hbm, w_dist), (bias_hbm, bias), (w_edge_hbm, w_edge), (w_gate_hbm, w_gate),
                (w_coord_hbm, w_coord), (w_weight_hbm, w_weight), (w_in_hbm, w_in), (w_out_hbm, w_out),
            ]
        )
    ]
    for copy in loads:
        copy.start()
    loads[0].wait()
    loads[1].wait()
    places = place[...]
    row = jnp.zeros((1, 128), F32)
    for k in range(3):
        row = row + dot(places[k : k + 1], (iota((16, 128), 0) + 16 * k == iota((16, 128), 1)).astype(BF16))
    place_row[...] = row
    pl.semaphore_wait(barrier, len(plane) + len(column))

    def send(source, target, k, peer):
        pltpu.make_async_remote_copy(
            source, target, send_sem.at[k], recv_sem.at[k], device_id=peer, device_id_type=MESH
        ).start()

    def wait(buffer, count, semaphore):
        part = buffer.at[pl.ds(0, count)]
        pltpu.make_async_copy(part, part, semaphore).wait()

    for peer in plane:
        send(feat, plane_feat.at[here], 0, peer)
        send(place_row, plane_place.at[here], 1, peer)
    for peer in near:
        send(feat, near_feat.at[edge], 2, peer)
        send(place_row, near_place.at[edge], 3, peer)
    plane_feat[here] = feat[...]
    plane_place[here] = row
    near_feat[edge] = feat[...]
    near_place[edge] = row

    for copy in loads[2:]:
        copy.wait()
    own_feat = feat[...]
    cols = [
        dot(places, (iota((3, 128), 0) == k).astype(BF16), ((0,), (0,))) for k in range(3)
    ]
    own_norm = cols[0] * cols[0] + cols[1] * cols[1] + cols[2] * cols[2]
    dist = w_dist[...]
    base = 0.5 * (dot(own_feat, w_tgt[...]) + bias[...] + own_norm * dist)
    cross = [split2(-c * dist) for c in cols]
    dist_high, dist_mid = split2(jnp.broadcast_to(0.5 * dist, (16, 128)))
    base_high, base_mid = split2(base)
    stack = [c[0] for c in cross] + [c[1] for c in cross]
    stack += [dist_high, dist_high, dist_mid, base_high, base_mid, dist_high]
    stack = jnp.concatenate(stack + [jnp.zeros((16, 128), BF16)] * (TERMS - len(stack)), axis=0)
    to, of = iota((256, 256), 0), iota((256, 256), 1)
    turned = dot((of == (to % 16) * 16 + to // 16).astype(BF16), stack).astype(BF16)
    src_half = w_src[...] * jnp.asarray(0.5, BF16)
    none = jnp.zeros((128, 128), BF16)
    for pair in range(8):
        wide[pair, :128, :128] = src_half
        wide[pair, :128, 128:] = src_half
        for side in range(2):
            at = (2 * pair + side) * 16
            wide[pair, 128:144, side * 128 : side * 128 + 128] = turned[at : at + 16]
        wide[pair, 144:, :] = jnp.zeros((112, 256), BF16)
    for full, part in ((edge_wide, w_edge), (coord_wide, w_coord)):
        halved = part[...] * jnp.asarray(0.5, BF16)
        full[:128, :128] = halved
        full[128:, 128:] = halved
        full[:128, 128:] = none
        full[128:, :128] = none

    def pieces(vector, factor):
        high, mid = split2(jnp.concatenate([vector * factor] * 2, axis=1))
        return high.astype(F32), mid.astype(F32)

    gate_row = pieces(w_gate[...], 0.5)
    weight_row = pieces(w_weight[...], 1.0)
    shared = (cols, wide, edge_wide[...], coord_wide[...], gate_row, weight_row)

    wait(near_feat, 7, recv_sem.at[2])
    wait(near_place, 7, recv_sem.at[3])
    for k in range(8):
        lhs[k * 16 : k * 16 + 16, :128] = near_feat[k]
        place_list[k : k + 1, :] = near_place[k]
    keep = (iota((16, 128), 1) != edge * 16 + iota((16, 128), 0)).astype(F32)
    message_own, coord_own = edge_sums(lhs, 0, 128, place_list[0:8, :], keep, *shared)

    wait(plane_feat, 31, recv_sem.at[0])
    wait(plane_place, 31, recv_sem.at[1])
    for side in range(2):
        for r in range(3):
            from_spot = table[r, here * 2 + side] // 2
            picked_feat[side, r] = plane_feat[from_spot]
            picked_place[side, r] = plane_place[from_spot]
    for peer, side in column:
        send(picked_feat.at[side], column_feat.at[spot], 4, peer)
        send(picked_place.at[side], column_place.at[spot], 5, peer)
    column_feat[spot] = picked_feat[z_hi]
    column_place[spot] = picked_place[z_hi]
    wait(column_feat, 15, recv_sem.at[4])
    wait(column_place, 15, recv_sem.at[5])
    for r in range(3):
        side = table[r, blk] % 2
        for k in range(8):
            at = r * 8 + k
            lhs[at * 16 : at * 16 + 16, :128] = column_feat[side * 8 + k, r]
            place_list[at : at + 1, :] = column_place[side * 8 + k, r]
    message_far, coord_far = edge_sums(lhs, 0, 384, place_list[...], None, *shared)

    mean_scale = 1.0 / 511
    mean = ((message_own + message_far) * mean_scale).astype(BF16)
    node_pre = dot(own_feat, w_in[:128, :]) + dot(mean, w_in[128:, :])
    node_hidden = (node_pre * jax.nn.sigmoid(node_pre)).astype(BF16)
    feat_out[...] = (own_feat.astype(F32) + dot(node_hidden, w_out[...])).astype(BF16)
    eye = iota((16, 16), 0) == iota((16, 16), 1)
    for k in range(3):
        moved = jnp.sum(jnp.where(eye, coord_own[k] + coord_far[k], 0.0), axis=0, keepdims=True)
        place_out[k : k + 1, :] = places[k : k + 1].astype(F32) + mean_scale * moved

    for k, buffer, count in (
        (0, plane_feat, 31), (1, plane_place, 31), (2, near_feat, 7), (3, near_place, 7),
        (4, column_feat, 15), (5, column_place, 15),
    ):
        wait(buffer, count, send_sem.at[k])


def shards(*args):
    args = [a.reshape(1, -1) if a.ndim == 1 else a for a in args]
    vmem = lambda shape, kind: pltpu.VMEM(shape, kind)
    loaded = [
        pltpu.SMEM(a.shape, a.dtype) if a.dtype == jnp.int32 else pltpu.VMEM(a.shape, a.dtype) for a in args
    ]
    return pl.pallas_call(
        layer,
        out_shape=(jax.ShapeDtypeStruct((ROWS, 128), BF16), jax.ShapeDtypeStruct((3, ROWS), F32)),
        in_specs=[pl.BlockSpec(memory_space=pl.ANY)] * len(args),
        out_specs=(pl.BlockSpec(memory_space=pltpu.VMEM), pl.BlockSpec(memory_space=pltpu.VMEM)),
        scratch_shapes=loaded
        + [
            vmem((1, 128), F32),
            vmem((8, 16, 128), BF16),
            vmem((8, 1, 128), F32),
            vmem((32, 16, 128), BF16),
            vmem((32, 1, 128), F32),
            vmem((2, 3, 16, 128), BF16),
            vmem((2, 3, 1, 128), F32),
            vmem((16, 3, 16, 128), BF16),
            vmem((16, 3, 1, 128), F32),
            vmem((384, 256), BF16),
            vmem((24, 128), F32),
            vmem((8, 256, 256), BF16),
            vmem((256, 256), BF16),
            vmem((256, 256), BF16),
            pltpu.SemaphoreType.DMA((13,)),
            pltpu.SemaphoreType.DMA((6,)),
            pltpu.SemaphoreType.DMA((6,)),
        ],
        compiler_params=pltpu.CompilerParams(
            collective_id=0, has_side_effects=True, vmem_limit_bytes=48 * 1024 * 1024
        ),
    )(*args)


def solution(mesh):
    specs = (P(("blk", "edge"), None), P(None, ("blk", "edge"))) + (P(),) * 11
    return jax.shard_map(
        shards,
        mesh=mesh,
        in_specs=specs,
        out_specs=(P(("blk", "edge"), None), P(None, ("blk", "edge"))),
        check_vma=False,
    )
```

time: 348 us -> 46.2 us (0.13)
  blocking collectives: 246 us -> 0 us
  Pallas kernels: 0 us -> 36.5 us
  waiting for transfers between devices: 32.7 us -> 0 us
  starting transfers between devices: 32.1 us -> 0 us
  other arithmetic: 10.4 us -> 0 us
  matrix products: 7.39 us -> 0 us
  between operations: 7.01 us -> 0.69 us
    all_gather x2 -> x0, blocking collectives: 246 us -> none  [the longest x1 203 us: in_one_piece(): filled = lax.all_gather(both, axis, axis=dim, tiled=True)]
    pallas_call x0 -> x1, Pallas kernels: none -> 36.5 us  [shards(): pl.pallas_call(layer, out_shape=(jax.ShapeDtypeStruct((ROWS, 128), BF16),...]
    all_to_all x8 -> x0, waiting for transfers between devices: 32.7 us -> none  [sent_and_summed(): blocks = lax.all_to_all(split_up(shard, dim, peers), axis, 0, 0, tiled=True)]
    all_to_all x8 -> x0, starting transfers between devices: 32.1 us -> none  [sent_and_summed(): blocks = lax.all_to_all(split_up(shard, dim, peers), axis, 0, 0, tiled=True)]
    dot_general x15 -> x0, matrix products: 7.39 us -> none  [the longest x4 3.11 us: edge_terms(): jnp.dot(hidden, w_edge, preferred_element_type=jnp.float32)]
    reduce_sum x15 -> x0, other arithmetic: 4.67 us -> none  [the longest x4 4.21 us: edge_terms(): jnp.sum(message.reshape(targets, sources, -1) * edge_gate[:, :, None], ax...]
    convert_element_type x5 -> x0, other arithmetic: 3.73 us -> none  [the longest x2 3.53 us: edge_terms(): jax.nn.silu(pre_act).astype(jnp.bfloat16).reshape(targets * sources, -1)]
    unnamed x34 -> x28, local copies, waits for them, and re-layouts: 5.69 us -> 8.44 us
  transfers between devices with their start and end apart: 8 -> 0, of which waited for: 8 -> 0; matrix products, arithmetic and copies ran while one was open for 2% -> 0% of each run, Pallas kernels for 0% -> 0%
where the time goes in v1:
time: 46.2 us; the launch traced here: 45.7 us
  Pallas kernels  36.5 us (79%)
  local copies, waits for them, and re-layouts  8.44 us (18%)
  between operations  0.69 us (1%)
    pallas_call x1, Pallas kernels, shards(): pl.pallas_call(layer, out_shape=(jax.ShapeDtypeStruct((ROWS, 128), BF16),...  36.5 us
    unnamed x28, local copies, waits for them, and re-layouts  8.44 us

profile of v1, /device:TPU:1, one launch (start us, length us, event | category | flops | bytes accessed | tf_op | source)
XLA Modules:
  0.0 45.7 jit_solution(3115335930482981514)
XLA Ops:
  0.6 0.0 copy-start.6
  0.6 0.0 copy-start.7
  0.7 0.0 copy-start.8
  0.7 0.0 copy-start.9
  0.7 0.6 %copy-done.6 = bf16[16,128]{1,0:T(8,128)(2,1)S(1)} copy-done((bf16[16,128]{1,0:T(8,128)(2,1)S(1)}, bf16[16,128]{1,0:T(8,128)(2,1)}, u32[]{:S(2)}) %copy-start.6) | copy-done | bytes 4120
  1.3 0.0 copy-done.7
  1.3 0.0 copy-done.8
  1.3 0.0 copy-done.9
  1.3 0.0 copy-start
  1.4 0.8 %copy-done = bf16[256,128]{1,0:T(8,128)(2,1)S(1)} copy-done((bf16[256,128]{1,0:T(8,128)(2,1)S(1)}, bf16[256,128]{1,0:T(8,128)(2,1)}, u32[]{:S(2)}) %copy-start) | copy-done | bytes 65560
  2.2 0.0 copy-start.1
  2.2 0.8 %copy-done.1 = bf16[128,128]{1,0:T(8,128)(2,1)S(1)} copy-done((bf16[128,128]{1,0:T(8,128)(2,1)S(1)}, bf16[128,128]{1,0:T(8,128)(2,1)}, u32[]{:S(2)}) %copy-start.1) | copy-done | bytes 32792
  2.9 0.0 copy-start.2
  3.0 0.8 %copy-done.2 = bf16[128,128]{1,0:T(8,128)(2,1)S(1)} copy-done((bf16[128,128]{1,0:T(8,128)(2,1)S(1)}, bf16[128,128]{1,0:T(8,128)(2,1)}, u32[]{:S(2)}) %copy-start.2) | copy-done | bytes 32792
  3.7 0.0 copy-start.3
  3.7 0.8 %copy-done.3 = bf16[128,128]{1,0:T(8,128)(2,1)S(1)} copy-done((bf16[128,128]{1,0:T(8,128)(2,1)S(1)}, bf16[128,128]{1,0:T(8,128)(2,1)}, u32[]{:S(2)}) %copy-start.3) | copy-done | bytes 32792
  4.5 0.0 copy-start.4
  4.5 0.8 %copy-done.4 = bf16[128,128]{1,0:T(8,128)(2,1)S(1)} copy-done((bf16[128,128]{1,0:T(8,128)(2,1)S(1)}, bf16[128,128]{1,0:T(8,128)(2,1)}, u32[]{:S(2)}) %copy-start.4) | copy-done | bytes 32792
  5.2 0.0 copy-start.5
  5.2 0.8 %copy-done.5 = bf16[128,128]{1,0:T(8,128)(2,1)S(1)} copy-done((bf16[128,128]{1,0:T(8,128)(2,1)S(1)}, bf16[128,128]{1,0:T(8,128)(2,1)}, u32[]{:S(2)}) %copy-start.5) | copy-done | bytes 32792
  6.0 0.0 copy-start.10
  6.0 0.7 %copy-done.10 = f32[128]{0:T(128)S(1)} copy-done((f32[128]{0:T(128)S(1)}, f32[128]{0:T(128)}, u32[]{:S(2)}) %copy-start.10) | copy-done | bytes 536
  6.6 0.0 copy-start.11
  6.6 0.7 %copy-done.11 = f32[128]{0:T(128)S(1)} copy-done((f32[128]{0:T(128)S(1)}, f32[128]{0:T(128)}, u32[]{:S(2)}) %copy-start.11) | copy-done | bytes 536
  7.3 0.0 copy-start.12
  7.3 0.7 %copy-done.12 = f32[128]{0:T(128)S(1)} copy-done((f32[128]{0:T(128)S(1)}, f32[128]{0:T(128)}, u32[]{:S(2)}) %copy-start.12) | copy-done | bytes 536
  7.9 36.5 %shard_map.140 = (bf16[16,128]{1,0:T(8,128)(2,1)S(1)}, f32[3,16]{1,0:T(4,128)S(1)}) custom-call(bf16[16,128]{1,0:T(8,128)(2,1)S(1)} %copy-done.6, bf16[3,16]{1,0:T(4,128)(2,1)S(1)} %copy-done.8, s32[3,64]{1,0:T(4,128)S(1)} %copy-done.7, bf16[128,128]{1,0:T(8,128)(2,1)S(1)} %copy-done.1, bf16[128,128]{1,0:T(8,128)(2,1)S(1)} %copy-done.2, ...), custom_call_target="tpu_custom_call" | custom-call | tf_op jit(solution)/shard_map/pallas_call | solution.py:255
  44.5 0.6 %copy.17 = bf16[16,128]{1,0:T(8,128)(2,1)} copy(bf16[16,128]{1,0:T(8,128)(2,1)S(1)} %get-tuple-element.4) | data formatting | bytes 8192
  45.1 0.6 %copy.18 = f32[3,16]{1,0:T(4,128)} copy(f32[3,16]{1,0:T(4,128)S(1)} %get-tuple-element.5) | data formatting | bytes 384
Async XLA Ops:
  0.6 0.7 %copy-start.6 = (bf16[16,128]{1,0:T(8,128)(2,1)S(1)}, bf16[16,128]{1,0:T(8,128)(2,1)}, u32[]{:S(2)}) copy-start(bf16[16,128]{1,0:T(8,128)(2,1)} %feat_hbm.1) | copy-start | bytes 12292
  0.6 0.7 %copy-start.7 = (s32[3,64]{1,0:T(4,128)S(1)}, s32[3,64]{1,0:T(4,128)}, u32[]{:S(2)}) copy-start(s32[3,64]{1,0:T(4,128)} %table_hbm.1) | copy-start | bytes 2308
  0.7 0.7 %copy-start.8 = (bf16[3,16]{1,0:T(4,128)(2,1)S(1)}, bf16[3,16]{1,0:T(4,128)(2,1)}, u32[]{:S(2)}) copy-start(bf16[3,16]{1,0:T(4,128)(2,1)} %place_hbm.1) | copy-start | bytes 292
  0.7 0.7 %copy-start.9 = (f32[128]{0:T(128)S(1)}, f32[128]{0:T(128)}, u32[]{:S(2)}) copy-start(f32[128]{0:T(128)} %param.18) | copy-start | bytes 1540
  1.3 0.8 %copy-start = (bf16[256,128]{1,0:T(8,128)(2,1)S(1)}, bf16[256,128]{1,0:T(8,128)(2,1)}, u32[]{:S(2)}) copy-start(bf16[256,128]{1,0:T(8,128)(2,1)} %w_in_hbm.1) | copy-start | bytes 196612
  2.2 0.8 %copy-start.1 = (bf16[128,128]{1,0:T(8,128)(2,1)S(1)}, bf16[128,128]{1,0:T(8,128)(2,1)}, u32[]{:S(2)}) copy-start(bf16[128,128]{1,0:T(8,128)(2,1)} %w_tgt_hbm.1) | copy-start | bytes 98308
  2.9 0.8 %copy-start.2 = (bf16[128,128]{1,0:T(8,128)(2,1)S(1)}, bf16[128,128]{1,0:T(8,128)(2,1)}, u32[]{:S(2)}) copy-start(bf16[128,128]{1,0:T(8,128)(2,1)} %w_src_hbm.1) | copy-start | bytes 98308
  3.7 0.8 %copy-start.3 = (bf16[128,128]{1,0:T(8,128)(2,1)S(1)}, bf16[128,128]{1,0:T(8,128)(2,1)}, u32[]{:S(2)}) copy-start(bf16[128,128]{1,0:T(8,128)(2,1)} %w_edge_hbm.1) | copy-start | bytes 98308
  4.5 0.8 %copy-start.4 = (bf16[128,128]{1,0:T(8,128)(2,1)S(1)}, bf16[128,128]{1,0:T(8,128)(2,1)}, u32[]{:S(2)}) copy-start(bf16[128,128]{1,0:T(8,128)(2,1)} %w_coord_hbm.1) | copy-start | bytes 98308
  5.2 0.8 %copy-start.5 = (bf16[128,128]{1,0:T(8,128)(2,1)S(1)}, bf16[128,128]{1,0:T(8,128)(2,1)}, u32[]{:S(2)}) copy-start(bf16[128,128]{1,0:T(8,128)(2,1)} %w_out_hbm.1) | copy-start | bytes 98308
  6.0 0.7 %copy-start.10 = (f32[128]{0:T(128)S(1)}, f32[128]{0:T(128)}, u32[]{:S(2)}) copy-start(f32[128]{0:T(128)} %param.19) | copy-start | bytes 1540
  6.6 0.7 %copy-start.11 = (f32[128]{0:T(128)S(1)}, f32[128]{0:T(128)}, u32[]{:S(2)}) copy-start(f32[128]{0:T(128)} %param.21) | copy-start | bytes 1540
  7.3 0.7 %copy-start.12 = (f32[128]{0:T(128)S(1)}, f32[128]{0:T(128)}, u32[]{:S(2)}) copy-start(f32[128]{0:T(128)} %param.23) | copy-start | bytes 1540

commit v2 on v1

--- a/solution.py
+++ b/solution.py
@@ -17,7 +17,7 @@
 COLUMN = [(dz, dc) for dz in RING[NZ] for dc in (1, 0) if dz or dc]
 EDGE = (4, 3, 5, 2, 6, 1, 7)
 ROWS = 16
-TERMS = 16
+TERMS = 32
 
 
 def iota(shape, dim):
@@ -37,58 +37,56 @@
     return h + h * jnp.tanh(h)
 
 
-def source_rows(places, count):
+def place_terms(places, count):
     slots = places.shape[0]
-    lane = iota((128, count), 0)
-    node = lax.rem(iota((128, count), 1), 16)
-    mine = (iota((slots, count), 1) // 16) == iota((slots, count), 0)
-    low = places.astype(BF16)
-    rows = []
-    for k in range(3):
-        spread = dot(low, (lane == node + 16 * k).astype(BF16))
-        rows.append(jnp.sum(jnp.where(mine, spread, 0.0), axis=0, keepdims=True))
-    return rows
-
-
-def edge_sums(lhs_ref, base, count, places, own, target_cols, wide_ref, w_edge2, w_coord2, gate_row, weight_row):
-    rows = source_rows(places, count)
-    norm = rows[0] * rows[0] + rows[1] * rows[1] + rows[2] * rows[2]
-    norm_high, norm_mid = split2(norm)
-    norm_low = (norm - norm_high.astype(F32) - norm_mid.astype(F32)).astype(F32)
-    one = jnp.ones((1, count), F32)
-    nh, nm = norm_high.astype(F32), norm_mid.astype(F32)
-    terms = rows + rows + [nh, nm, nh, one, one, norm_low]
-    terms = jnp.concatenate(terms + [jnp.zeros((TERMS - len(terms), count), F32)], axis=0).astype(BF16)
-    place_term = (iota((TERMS, 128), 0) == iota((TERMS, 128), 1)).astype(BF16)
-    lhs_ref[pl.ds(base, count), 128:256] = dot(terms, place_term, ((0,), (0,))).astype(BF16)
-    lhs = lhs_ref[pl.ds(base, count), :]
-
-    offsets = [target_cols[k][:, :1] - rows[k] for k in range(3)]
+    spread = jnp.broadcast_to(places[:, None, :], (slots, 16, 128)).reshape(count, 128)
+    lane, node = iota((count, 128), 1), lax.rem(iota((count, 128), 0), 16)
+    spread = jnp.where(lax.rem(lane, 16) == node, spread, 0.0)
+    square_high, square_low = split2(spread * spread)
+    parts = jnp.concatenate([spread.astype(BF16), square_high, square_low], axis=1)
+    row, term = iota((384, 128), 0), iota((384, 128), 1)
+    axis = lax.rem(row, 128) // 16
+    kind = row // 128
+    first = jnp.where(kind == 0, 0, 6 * kind)
+    hit = (term == first + axis) | ((kind < 2) & (term == first + 3 + axis))
+    placed = dot(parts, ((axis < 3) & hit).astype(BF16))
+    ones = (lane == 15) | (lane == 16)
+    return jnp.where(ones, 1.0, placed).astype(BF16)
+
+
+def edge_sums(feats, places, count, own, target_cols, wide, w_edge2, w_coord2, gate_pick, weight_pick, hidden, message, lifted):
+    terms = place_terms(places, count)
+    chunks = [(at, pair) for pair in range(8) for at in range(0, count, 128)]
+    lhs = [jnp.concatenate([feats(at), terms[at : at + 128]], axis=1) for at in range(0, count, 128)]
+    for at, pair in chunks:
+        half = dot(lhs[at // 128], wide[pair]).astype(BF16)
+        hidden[at : at + 128, pair * 256 : pair * 256 + 256] = half_silu(half)
+
+    rows8 = dot((iota((8, 128), 0) == iota((8, 128), 1)).astype(BF16), terms, ((1,), (1,)))
+    offsets = [target_cols[k][:, :1] - rows8[k : k + 1] for k in range(3)]
     radial = offsets[0] * offsets[0] + offsets[1] * offsets[1] + offsets[2] * offsets[2]
     scale = 1.0 / (jnp.sqrt(radial) + 1.0)
 
-    row16, col16 = iota((16, 256), 0), iota((16, 256), 1)
-    message_sum = jnp.zeros((16, 256), F32)
-    weights = jnp.zeros((16, count), F32)
-    for pair in range(8):
-        half = dot(lhs, wide_ref[pair]).astype(BF16)
-        hidden = half_silu(half)
-        message = half_silu(dot(hidden, w_edge2).astype(BF16))
-        lifted = half_silu(dot(message, w_coord2).astype(BF16))
-        here = row16 == 2 * pair + col16 // 128
-        pick = lambda pieces: jnp.concatenate([jnp.where(here, p, 0.0) for p in pieces], axis=0).astype(BF16)
-        logit = dot(pick(gate_row), message, ((1,), (1,)))
-        gate = 0.5 + 0.5 * jnp.tanh(logit[:16] + logit[16:])
-        if own is not None:
-            gate = gate * own
-        message_sum = message_sum + jnp.where(here, dot(gate.astype(BF16), message), 0.0)
-        weight = dot(pick(weight_row), lifted, ((1,), (1,)))
-        weights = weights + (weight[:16] + weight[16:])
+    for at, pair in chunks:
+        half = dot(hidden[at : at + 128, pair * 256 : pair * 256 + 256], w_edge2).astype(BF16)
+        message[at : at + 128, pair * 256 : pair * 256 + 256] = half_silu(half)
+    for at, pair in chunks:
+        half = dot(message[at : at + 128, pair * 256 : pair * 256 + 256], w_coord2).astype(BF16)
+        lifted[at : at + 128, pair * 256 : pair * 256 + 256] = half_silu(half)
+    messages = message[:count, :]
+    logit = dot(gate_pick[...], messages, ((1,), (1,)))
+    gate = 0.5 + 0.5 * jnp.tanh(logit[:16] + logit[16:])
+    weight = dot(weight_pick[...], lifted[:count, :], ((1,), (1,)))
+    weight = (weight[:16] + weight[16:]) * scale
     if own is not None:
-        weights = weights * own
-    weights = weights * scale
-    coord_sum = [jnp.sum(offsets[k] * weights, axis=1, keepdims=True) for k in range(3)]
-    return message_sum[:, :128] + message_sum[:, 128:], coord_sum
+        gate, weight = gate * own, weight * own
+    spread = dot(gate.astype(BF16), messages)
+    row = iota((16, 128), 0)
+    message_sum = jnp.zeros((16, 128), F32)
+    for i in range(16):
+        message_sum = message_sum + jnp.where(row == i, spread[:, i * 128 : i * 128 + 128], 0.0)
+    coord_sum = [jnp.sum(offsets[k] * weight, axis=1, keepdims=True) for k in range(3)]
+    return message_sum, coord_sum
 
 
 def layer(
@@ -97,7 +95,8 @@
     feat_out, place_out,
     feat, place, table, w_tgt, w_src, w_dist, bias, w_edge, w_gate, w_coord, w_weight, w_in, w_out,
     place_row, near_feat, near_place, plane_feat, plane_place, picked_feat, picked_place,
-    column_feat, column_place, lhs, place_list, wide, edge_wide, coord_wide,
+    column_feat, column_place, lhs, place_list, wide, edge_wide, coord_wide, gate_pick, weight_pick,
+    hidden, message, lifted,
     load_sem, send_sem, recv_sem,
 ):
     blk, edge = lax.axis_index("blk"), lax.axis_index("edge")
@@ -171,19 +170,19 @@
     dist_high, dist_mid = split2(jnp.broadcast_to(0.5 * dist, (16, 128)))
     base_high, base_mid = split2(base)
     stack = [c[0] for c in cross] + [c[1] for c in cross]
-    stack += [dist_high, dist_high, dist_mid, base_high, base_mid, dist_high]
+    stack += [dist_high] * 3 + [dist_mid] * 3 + [dist_high] * 3 + [base_high, base_mid]
     stack = jnp.concatenate(stack + [jnp.zeros((16, 128), BF16)] * (TERMS - len(stack)), axis=0)
-    to, of = iota((256, 256), 0), iota((256, 256), 1)
-    turned = dot((of == (to % 16) * 16 + to // 16).astype(BF16), stack).astype(BF16)
+    to, of = iota((512, 512), 0), iota((512, 512), 1)
+    turned = dot((of == (to % TERMS) * 16 + to // TERMS).astype(BF16), stack).astype(BF16)
     src_half = w_src[...] * jnp.asarray(0.5, BF16)
     none = jnp.zeros((128, 128), BF16)
     for pair in range(8):
         wide[pair, :128, :128] = src_half
         wide[pair, :128, 128:] = src_half
         for side in range(2):
-            at = (2 * pair + side) * 16
-            wide[pair, 128:144, side * 128 : side * 128 + 128] = turned[at : at + 16]
-        wide[pair, 144:, :] = jnp.zeros((112, 256), BF16)
+            at = (2 * pair + side) * TERMS
+            wide[pair, 128 : 128 + TERMS, side * 128 : side * 128 + 128] = turned[at : at + TERMS]
+        wide[pair, 128 + TERMS :, :] = jnp.zeros((128 - TERMS, 256), BF16)
     for full, part in ((edge_wide, w_edge), (coord_wide, w_coord)):
         halved = part[...] * jnp.asarray(0.5, BF16)
         full[:128, :128] = halved
@@ -191,21 +190,20 @@
         full[:128, 128:] = none
         full[128:, :128] = none
 
-    def pieces(vector, factor):
-        high, mid = split2(jnp.concatenate([vector * factor] * 2, axis=1))
-        return high.astype(F32), mid.astype(F32)
-
-    gate_row = pieces(w_gate[...], 0.5)
-    weight_row = pieces(w_weight[...], 1.0)
-    shared = (cols, wide, edge_wide[...], coord_wide[...], gate_row, weight_row)
+    mine = iota((16, 2048), 0) == iota((16, 2048), 1) // 128
+    for pick, vector in ((gate_pick, 0.5 * w_gate[...]), (weight_pick, w_weight[...])):
+        for side, part in enumerate(split2(vector)):
+            part = jnp.concatenate([part.astype(F32)] * 16, axis=1)
+            pick[side * 16 : side * 16 + 16, :] = jnp.where(mine, part, 0.0).astype(BF16)
+    shared = (cols, wide, edge_wide[...], coord_wide[...], gate_pick, weight_pick, hidden, message, lifted)
 
     wait(near_feat, 7, recv_sem.at[2])
     wait(near_place, 7, recv_sem.at[3])
     for k in range(8):
-        lhs[k * 16 : k * 16 + 16, :128] = near_feat[k]
         place_list[k : k + 1, :] = near_place[k]
     keep = (iota((16, 128), 1) != edge * 16 + iota((16, 128), 0)).astype(F32)
-    message_own, coord_own = edge_sums(lhs, 0, 128, place_list[0:8, :], keep, *shared)
+    near_rows = lambda at: near_feat[...].reshape(128, 128)
+    message_own, coord_own = edge_sums(near_rows, place_list[0:8, :], 128, keep, *shared)
 
     wait(plane_feat, 31, recv_sem.at[0])
     wait(plane_place, 31, recv_sem.at[1])
@@ -225,9 +223,10 @@
         side = table[r, blk] % 2
         for k in range(8):
             at = r * 8 + k
-            lhs[at * 16 : at * 16 + 16, :128] = column_feat[side * 8 + k, r]
+            lhs[at * 16 : at * 16 + 16, :] = column_feat[side * 8 + k, r]
             place_list[at : at + 1, :] = column_place[side * 8 + k, r]
-    message_far, coord_far = edge_sums(lhs, 0, 384, place_list[...], None, *shared)
+    far_rows = lambda at: lhs[at : at + 128, :]
+    message_far, coord_far = edge_sums(far_rows, place_list[...], 384, None, *shared)
 
     mean_scale = 1.0 / 511
     mean = ((message_own + message_far) * mean_scale).astype(BF16)
@@ -255,7 +254,7 @@
     return pl.pallas_call(
         layer,
         out_shape=(jax.ShapeDtypeStruct((ROWS, 128), BF16), jax.ShapeDtypeStruct((3, ROWS), F32)),
-        in_specs=[pl.BlockSpec(memory_space=pl.ANY)] * len(args),
+        in_specs=[pl.BlockSpec(memory_space=pltpu.HBM)] * len(args),
         out_specs=(pl.BlockSpec(memory_space=pltpu.VMEM), pl.BlockSpec(memory_space=pltpu.VMEM)),
         scratch_shapes=loaded
         + [
@@ -268,17 +267,22 @@
             vmem((2, 3, 1, 128), F32),
             vmem((16, 3, 16, 128), BF16),
             vmem((16, 3, 1, 128), F32),
-            vmem((384, 256), BF16),
+            vmem((384, 128), BF16),
             vmem((24, 128), F32),
             vmem((8, 256, 256), BF16),
             vmem((256, 256), BF16),
             vmem((256, 256), BF16),
+            vmem((32, 2048), BF16),
+            vmem((32, 2048), BF16),
+            vmem((384, 2048), BF16),
+            vmem((384, 2048), BF16),
+            vmem((384, 2048), BF16),
             pltpu.SemaphoreType.DMA((13,)),
             pltpu.SemaphoreType.DMA((6,)),
             pltpu.SemaphoreType.DMA((6,)),
         ],
         compiler_params=pltpu.CompilerParams(
-            collective_id=0, has_side_effects=True, vmem_limit_bytes=48 * 1024 * 1024
+            collective_id=0, has_side_effects=True, vmem_limit_bytes=60 * 1024 * 1024
         ),
     )(*args)
 

time: 46.2 us -> 35.4 us (0.77)
  local copies, waits for them, and re-layouts: 8.44 us -> 1.85 us
  Pallas kernels: 36.5 us -> 32.7 us
    unnamed x28 -> x4, local copies, waits for them, and re-layouts: 8.44 us -> 1.85 us
    pallas_call x1, Pallas kernels: 36.5 us -> 32.7 us  [shards(): pl.pallas_call(layer, out_shape=(jax.ShapeDtypeStruct((ROWS, 128), BF16),...]
where the time goes in v2:
time: 35.4 us; the launch traced here: 35.2 us
  Pallas kernels  32.7 us (92%)
  local copies, waits for them, and re-layouts  1.85 us (5%)
  between operations  0.65 us (2%)
    pallas_call x1, Pallas kernels, shards(): pl.pallas_call(layer, out_shape=(jax.ShapeDtypeStruct((ROWS, 128), BF16),...  32.7 us
    unnamed x4, local copies, waits for them, and re-layouts  1.85 us

profile of v2, /device:TPU:1, one launch (start us, length us, event | category | flops | bytes accessed | tf_op | source)
XLA Modules:
  0.0 35.2 jit_solution(7734117315672028204)
XLA Ops:
  0.6 32.7 %shard_map.140 = (bf16[16,128]{1,0:T(8,128)(2,1)}, f32[3,16]{1,0:T(4,128)}) custom-call(bf16[16,128]{1,0:T(8,128)(2,1)} %feat_hbm.1, bf16[3,16]{1,0:T(4,128)(2,1)} %place_hbm.1, s32[3,64]{1,0:T(4,128)} %table_hbm.1, bf16[128,128]{1,0:T(8,128)(2,1)} %w_tgt_hbm.1, bf16[128,128]{1,0:T(8,128)(2,1)} %w_src_hbm.1, f32[1,128]{1,0:T(1,128)} %bitcast.4, ...), custom_call_target="tpu_custom_call" | custom-call | tf_op jit(solution)/shard_map/pallas_call | solution.py:254
  33.4 0.0 copy-start
  33.4 1.3 %copy.17 = bf16[16,128]{1,0:T(8,128)(2,1)} copy(bf16[16,128]{1,0:T(8,128)(2,1)} %get-tuple-element.4) | data formatting | bytes 8192
  34.7 0.0 copy-done
  34.7 0.6 %copy.18 = f32[3,16]{1,0:T(4,128)} copy(f32[3,16]{1,0:T(4,128)S(1)} %copy-done) | data formatting | bytes 384
Async XLA Ops:
  33.4 1.3 %copy-start = (f32[3,16]{1,0:T(4,128)S(1)}, f32[3,16]{1,0:T(4,128)}, u32[]{:S(2)}) copy-start(f32[3,16]{1,0:T(4,128)} %get-tuple-element.5) | copy-start | bytes 580

commit v3 on v2

--- a/solution.py
+++ b/solution.py
@@ -197,6 +197,22 @@
             pick[side * 16 : side * 16 + 16, :] = jnp.where(mine, part, 0.0).astype(BF16)
     shared = (cols, wide, edge_wide[...], coord_wide[...], gate_pick, weight_pick, hidden, message, lifted)
 
+    wait(plane_feat, 31, recv_sem.at[0])
+    wait(plane_place, 31, recv_sem.at[1])
+    for side in range(2):
+        for r in range(3):
+            from_spot = table[r, here * 2 + side] // 2
+            picked_feat[side, r] = plane_feat[from_spot]
+            picked_place[side, r] = plane_place[from_spot]
+    for z_to in range(NZ):
+      for c_to in range(2):
+        @pl.when(spot != z_to * 2 + c_to)
+        def _(z_to=z_to, c_to=c_to):
+            peer = {"blk": here * 2 + z_to // 4, "edge": (z_to % 4) * 2 + c_to}
+            send(picked_feat.at[z_to // 4], column_feat.at[spot], 4, peer)
+            send(picked_place.at[z_to // 4], column_place.at[spot], 5, peer)
+    column_feat[spot] = picked_feat[z_hi]
+    column_place[spot] = picked_place[z_hi]
     wait(near_feat, 7, recv_sem.at[2])
     wait(near_place, 7, recv_sem.at[3])
     for k in range(8):
@@ -205,18 +221,6 @@
     near_rows = lambda at: near_feat[...].reshape(128, 128)
     message_own, coord_own = edge_sums(near_rows, place_list[0:8, :], 128, keep, *shared)
 
-    wait(plane_feat, 31, recv_sem.at[0])
-    wait(plane_place, 31, recv_sem.at[1])
-    for side in range(2):
-        for r in range(3):
-            from_spot = table[r, here * 2 + side] // 2
-            picked_feat[side, r] = plane_feat[from_spot]
-            picked_place[side, r] = plane_place[from_spot]
-    for peer, side in column:
-        send(picked_feat.at[side], column_feat.at[spot], 4, peer)
-        send(picked_place.at[side], column_place.at[spot], 5, peer)
-    column_feat[spot] = picked_feat[z_hi]
-    column_place[spot] = picked_place[z_hi]
     wait(column_feat, 15, recv_sem.at[4])
     wait(column_place, 15, recv_sem.at[5])
     for r in range(3):
@@ -251,9 +255,10 @@
     loaded = [
         pltpu.SMEM(a.shape, a.dtype) if a.dtype == jnp.int32 else pltpu.VMEM(a.shape, a.dtype) for a in args
     ]
+    args = [pltpu.with_memory_space_constraint(a, pltpu.HBM) for a in args]
     return pl.pallas_call(
         layer,
-        out_shape=(jax.ShapeDtypeStruct((ROWS, 128), BF16), jax.ShapeDtypeStruct((3, ROWS), F32)),
+        out_shape=(pltpu.VMEM((ROWS, 128), BF16), pltpu.VMEM((3, ROWS), F32)),
         in_specs=[pl.BlockSpec(memory_space=pltpu.HBM)] * len(args),
         out_specs=(pl.BlockSpec(memory_space=pltpu.VMEM), pl.BlockSpec(memory_space=pltpu.VMEM)),
         scratch_shapes=loaded
@@ -282,7 +287,7 @@
             pltpu.SemaphoreType.DMA((6,)),
         ],
         compiler_params=pltpu.CompilerParams(
-            collective_id=0, has_side_effects=True, vmem_limit_bytes=60 * 1024 * 1024
+            collective_id=0, has_side_effects=True, vmem_limit_bytes=40 * 1024 * 1024
         ),
     )(*args)
 

time: 35.4 us -> 32.6 us (0.921)
  Pallas kernels: 32.7 us -> 30.6 us
  local copies, waits for them, and re-layouts: 1.85 us -> 1.17 us
    pallas_call x1, Pallas kernels: 32.7 us -> 30.6 us  [shards(): pl.pallas_call(layer, out_shape=(pltpu.VMEM((ROWS, 128), BF16), pltpu.VME...]
    unnamed x4 -> x2, local copies, waits for them, and re-layouts: 1.85 us -> 1.17 us
where the time goes in v3:
time: 32.6 us; the launch traced here: 32.4 us
  Pallas kernels  30.6 us (94%)
  local copies, waits for them, and re-layouts  1.17 us (4%)
  between operations  0.64 us (2%)
    pallas_call x1, Pallas kernels, shards(): pl.pallas_call(layer, out_shape=(pltpu.VMEM((ROWS, 128), BF16), pltpu.VME...  30.6 us
    unnamed x2, local copies, waits for them, and re-layouts  1.17 us

profile of v3, /device:TPU:1, one launch (start us, length us, event | category | flops | bytes accessed | tf_op | source)
XLA Modules:
  0.0 32.4 jit_solution(1036782015595822066)
XLA Ops:
  0.6 30.6 %shard_map.140 = (bf16[16,128]{1,0:T(8,128)(2,1)S(1)}, f32[3,16]{1,0:T(4,128)S(1)}) custom-call(bf16[16,128]{1,0:T(8,128)(2,1)} %feat_hbm.1, bf16[3,16]{1,0:T(4,128)(2,1)} %place_hbm.1, s32[3,64]{1,0:T(4,128)} %table_hbm.1, bf16[128,128]{1,0:T(8,128)(2,1)} %w_tgt_hbm.1, bf16[128,128]{1,0:T(8,128)(2,1)} %w_src_hbm.1, f32[1,128]{1,0:T(1,128)} %bitcast.4, ...), custom_call_target="tpu_custom_call" | custom-call | tf_op jit(solution)/shard_map/pallas_call | solution.py:259
  31.3 0.6 %copy.17 = bf16[16,128]{1,0:T(8,128)(2,1)} copy(bf16[16,128]{1,0:T(8,128)(2,1)S(1)} %get-tuple-element.2) | data formatting | bytes 8192
  31.9 0.6 %copy.18 = f32[3,16]{1,0:T(4,128)} copy(f32[3,16]{1,0:T(4,128)S(1)} %get-tuple-element.3) | data formatting | bytes 384

commit v4 on v3

--- a/solution.py
+++ b/solution.py
@@ -249,6 +249,17 @@
         wait(buffer, count, send_sem.at[k])
 
 
+def deliver(feat_in, place_in, feat_out, place_out, sems):
+    copies = [
+        pltpu.make_async_copy(feat_in, feat_out, sems.at[0]),
+        pltpu.make_async_copy(place_in, place_out, sems.at[1]),
+    ]
+    for copy in copies:
+        copy.start()
+    for copy in copies:
+        copy.wait()
+
+
 def shards(*args):
     args = [a.reshape(1, -1) if a.ndim == 1 else a for a in args]
     vmem = lambda shape, kind: pltpu.VMEM(shape, kind)
@@ -256,7 +267,7 @@
         pltpu.SMEM(a.shape, a.dtype) if a.dtype == jnp.int32 else pltpu.VMEM(a.shape, a.dtype) for a in args
     ]
     args = [pltpu.with_memory_space_constraint(a, pltpu.HBM) for a in args]
-    return pl.pallas_call(
+    results = pl.pallas_call(
         layer,
         out_shape=(pltpu.VMEM((ROWS, 128), BF16), pltpu.VMEM((3, ROWS), F32)),
         in_specs=[pl.BlockSpec(memory_space=pltpu.HBM)] * len(args),
@@ -290,6 +301,13 @@
             collective_id=0, has_side_effects=True, vmem_limit_bytes=40 * 1024 * 1024
         ),
     )(*args)
+    return pl.pallas_call(
+        deliver,
+        out_shape=(jax.ShapeDtypeStruct((ROWS, 128), BF16), jax.ShapeDtypeStruct((3, ROWS), F32)),
+        in_specs=[pl.BlockSpec(memory_space=pltpu.VMEM)] * 2,
+        out_specs=(pl.BlockSpec(memory_space=pltpu.HBM),) * 2,
+        scratch_shapes=[pltpu.SemaphoreType.DMA((2,))],
+    )(*[pltpu.with_memory_space_constraint(r, pltpu.VMEM) for r in results])
 
 
 def solution(mesh):

time: 32.6 us -> 32 us (0.982)
  local copies, waits for them, and re-layouts: 1.17 us -> 0 us
  Pallas kernels: 30.6 us -> 31.2 us
    unnamed x2 -> x0, local copies, waits for them, and re-layouts: 1.17 us -> none
    pallas_call x0 -> x1, Pallas kernels: none -> 0.61 us  [shards(): pl.pallas_call(deliver, out_shape=(jax.ShapeDtypeStruct((ROWS, 128), BF16...]
where the time goes in v4:
time: 32 us; the launch traced here: 31.9 us
  Pallas kernels  31.2 us (98%)
  between operations  0.64 us (2%)
    pallas_call x1, Pallas kernels, shards(): pl.pallas_call(layer, out_shape=(pltpu.VMEM((ROWS, 128), BF16), pltpu.VME...  30.6 us

profile of v4, /device:TPU:1, one launch (start us, length us, event | category | flops | bytes accessed | tf_op | source)
XLA Modules:
  0.0 31.9 jit_solution(839664318221321034)
XLA Ops:
  0.6 30.6 %shard_map.140 = (bf16[16,128]{1,0:T(8,128)(2,1)S(1)}, f32[3,16]{1,0:T(4,128)S(1)}) custom-call(bf16[16,128]{1,0:T(8,128)(2,1)} %feat_hbm.1, bf16[3,16]{1,0:T(4,128)(2,1)} %place_hbm.1, s32[3,64]{1,0:T(4,128)} %table_hbm.1, bf16[128,128]{1,0:T(8,128)(2,1)} %w_tgt_hbm.1, bf16[128,128]{1,0:T(8,128)(2,1)} %w_src_hbm.1, f32[1,128]{1,0:T(1,128)} %bitcast.4, ...), custom_call_target="tpu_custom_call" | custom-call | tf_op jit(solution)/shard_map/pallas_call | solution.py:270
  31.3 0.6 %shard_map.141 = (bf16[16,128]{1,0:T(8,128)(2,1)}, f32[3,16]{1,0:T(4,128)}) custom-call(bf16[16,128]{1,0:T(8,128)(2,1)S(1)} %get-tuple-element.4.feat_in, f32[3,16]{1,0:T(4,128)S(1)} %get-tuple-element.5.place_in), custom_call_target="tpu_custom_call" | custom-call | tf_op jit(solution)/shard_map/pallas_call | solution.py:304

commit v5 on v4

--- a/solution.py
+++ b/solution.py
@@ -14,7 +14,6 @@
 NX, NY, NZ = 4, 8, 8
 RING = {4: (2, 1, 3, 0), 8: (4, 3, 5, 2, 6, 1, 7, 0)}
 PLANE = [(dx, dy) for dx in RING[NX] for dy in RING[NY] if dx or dy]
-COLUMN = [(dz, dc) for dz in RING[NZ] for dc in (1, 0) if dz or dc]
 EDGE = (4, 3, 5, 2, 6, 1, 7)
 ROWS = 16
 TERMS = 32
@@ -97,7 +96,7 @@
     place_row, near_feat, near_place, plane_feat, plane_place, picked_feat, picked_place,
     column_feat, column_place, lhs, place_list, wide, edge_wide, coord_wide, gate_pick, weight_pick,
     hidden, message, lifted,
-    load_sem, send_sem, recv_sem,
+    load_sem, send_sem, recv_sem, ready_sem,
 ):
     blk, edge = lax.axis_index("blk"), lax.axis_index("edge")
     x, y, z_hi = blk // 16, (blk // 2) % 8, blk % 2
@@ -107,15 +106,9 @@
     spot = z * 2 + core
 
     plane = [{"blk": (lax.rem(x + dx, NX) * NY + lax.rem(y + dy, NY)) * 2 + z_hi} for dx, dy in PLANE]
-    column = []
-    for dz, dc in COLUMN:
-        z_to = lax.rem(z + dz, NZ)
-        column.append(({"blk": here * 2 + z_to // 4, "edge": (z_to % 4) * 2 + lax.rem(core + dc, 2)}, z_to // 4))
+    across = [{"blk": here * 2 + 1 - z_hi, "edge": k} for k in range(8)]
     near = [{"edge": lax.rem(edge + step, 8)} for step in EDGE]
 
-    barrier = pltpu.get_barrier_semaphore()
-    for peer in plane + [c[0] for c in column]:
-        pl.semaphore_signal(barrier, inc=1, device_id=peer, device_id_type=MESH)
     loads = [
         pltpu.make_async_copy(a, b, load_sem.at[k])
         for k, (a, b) in enumerate(
@@ -126,8 +119,17 @@
             ]
         )
     ]
-    for copy in loads:
-        copy.start()
+    loads[0].start()
+    loads[1].start()
+    barrier = pltpu.get_barrier_semaphore()
+    for peer in plane + near:
+        pl.semaphore_signal(barrier, inc=1, device_id=peer, device_id_type=MESH)
+
+    @pl.when(z_hi == 0)
+    def _():
+        for peer in across:
+            pl.semaphore_signal(barrier, inc=1, device_id=peer, device_id_type=MESH)
+
     loads[0].wait()
     loads[1].wait()
     places = place[...]
@@ -135,7 +137,7 @@
     for k in range(3):
         row = row + dot(places[k : k + 1], (iota((16, 128), 0) + 16 * k == iota((16, 128), 1)).astype(BF16))
     place_row[...] = row
-    pl.semaphore_wait(barrier, len(plane) + len(column))
+    pl.semaphore_wait(barrier, len(plane) + len(near) + len(across) * z_hi)
 
     def send(source, target, k, peer):
         pltpu.make_async_remote_copy(
@@ -149,6 +151,13 @@
     for peer in plane:
         send(feat, plane_feat.at[here], 0, peer)
         send(place_row, plane_place.at[here], 1, peer)
+    @pl.when(z_hi == 1)
+    def _():
+        for peer in across:
+            pl.semaphore_signal(ready_sem, inc=1, device_id=peer, device_id_type=MESH)
+
+    for copy in loads[2:]:
+        copy.start()
     for peer in near:
         send(feat, near_feat.at[edge], 2, peer)
         send(place_row, near_place.at[edge], 3, peer)
@@ -204,13 +213,18 @@
             from_spot = table[r, here * 2 + side] // 2
             picked_feat[side, r] = plane_feat[from_spot]
             picked_place[side, r] = plane_place[from_spot]
-    for z_to in range(NZ):
-      for c_to in range(2):
-        @pl.when(spot != z_to * 2 + c_to)
-        def _(z_to=z_to, c_to=c_to):
-            peer = {"blk": here * 2 + z_to // 4, "edge": (z_to % 4) * 2 + c_to}
-            send(picked_feat.at[z_to // 4], column_feat.at[spot], 4, peer)
-            send(picked_place.at[z_to // 4], column_place.at[spot], 5, peer)
+    for to in range(16):
+        if to == 8:
+
+            @pl.when(z_hi == 0)
+            def _():
+                pl.semaphore_wait(ready_sem, 8)
+
+        @pl.when(spot != to)
+        def _(to=to):
+            peer = {"blk": here * 2 + to // 8, "edge": to % 8}
+            send(picked_feat.at[to // 8], column_feat.at[spot], 4, peer)
+            send(picked_place.at[to // 8], column_place.at[spot], 5, peer)
     column_feat[spot] = picked_feat[z_hi]
     column_place[spot] = picked_place[z_hi]
     wait(near_feat, 7, recv_sem.at[2])
@@ -296,6 +310,7 @@
             pltpu.SemaphoreType.DMA((13,)),
             pltpu.SemaphoreType.DMA((6,)),
             pltpu.SemaphoreType.DMA((6,)),
+            pltpu.SemaphoreType.REGULAR,
         ],
         compiler_params=pltpu.CompilerParams(
             collective_id=0, has_side_effects=True, vmem_limit_bytes=40 * 1024 * 1024

time: 32 us -> 31.7 us (level)
  Pallas kernels: 31.2 us -> 30.8 us
    pallas_call x1, Pallas kernels: 30.6 us -> 30.2 us  [shards(): pl.pallas_call(layer, out_shape=(pltpu.VMEM((ROWS, 128), BF16), pltpu.VME...]
where the time goes in v5:
time: 31.7 us; the launch traced here: 31.5 us
  Pallas kernels  30.8 us (97%)
  between operations  0.64 us (2%)
    pallas_call x1, Pallas kernels, shards(): pl.pallas_call(layer, out_shape=(pltpu.VMEM((ROWS, 128), BF16), pltpu.VME...  30.2 us

profile of v5, /device:TPU:1, one launch (start us, length us, event | category | flops | bytes accessed | tf_op | source)
XLA Modules:
  0.0 31.5 jit_solution(9938166467398803048)
XLA Ops:
  0.6 30.2 %shard_map.140 = (bf16[16,128]{1,0:T(8,128)(2,1)S(1)}, f32[3,16]{1,0:T(4,128)S(1)}) custom-call(bf16[16,128]{1,0:T(8,128)(2,1)} %feat_hbm.1, bf16[3,16]{1,0:T(4,128)(2,1)} %place_hbm.1, s32[3,64]{1,0:T(4,128)} %table_hbm.1, bf16[128,128]{1,0:T(8,128)(2,1)} %w_tgt_hbm.1, bf16[128,128]{1,0:T(8,128)(2,1)} %w_src_hbm.1, f32[1,128]{1,0:T(1,128)} %bitcast.4, ...), custom_call_target="tpu_custom_call" | custom-call | tf_op jit(solution)/shard_map/pallas_call | solution.py:284
  30.9 0.6 %shard_map.141 = (bf16[16,128]{1,0:T(8,128)(2,1)}, f32[3,16]{1,0:T(4,128)}) custom-call(bf16[16,128]{1,0:T(8,128)(2,1)S(1)} %get-tuple-element.4.feat_in, f32[3,16]{1,0:T(4,128)S(1)} %get-tuple-element.5.place_in), custom_call_target="tpu_custom_call" | custom-call | tf_op jit(solution)/shard_map/pallas_call | solution.py:319

commit v6 on v5

--- a/solution.py
+++ b/solution.py
@@ -148,9 +148,14 @@
         part = buffer.at[pl.ds(0, count)]
         pltpu.make_async_copy(part, part, semaphore).wait()
 
-    for peer in plane:
-        send(feat, plane_feat.at[here], 0, peer)
-        send(place_row, plane_place.at[here], 1, peer)
+    for px, py in sorted(((a, b) for a in range(NX) for b in range(NY)), key=lambda q: min(q[0], NX - q[0]) + min(q[1], NY - q[1])):
+
+        @pl.when(here != px * NY + py)
+        def _(px=px, py=py):
+            peer = {"blk": (px * NY + py) * 2 + z_hi}
+            send(feat, plane_feat.at[here], 0, peer)
+            send(place_row, plane_place.at[here], 1, peer)
+
     @pl.when(z_hi == 1)
     def _():
         for peer in across:

time: 31.7 us -> 31.1 us (0.981)
  Pallas kernels: 30.8 us -> 30.2 us
    pallas_call x1, Pallas kernels: 30.2 us -> 29.6 us  [shards(): pl.pallas_call(layer, out_shape=(pltpu.VMEM((ROWS, 128), BF16), pltpu.VME...]
where the time goes in v6:
time: 31.1 us; the launch traced here: 30.9 us
  Pallas kernels  30.2 us (97%)
  between operations  0.64 us (2%)
    pallas_call x1, Pallas kernels, shards(): pl.pallas_call(layer, out_shape=(pltpu.VMEM((ROWS, 128), BF16), pltpu.VME...  29.6 us

profile of v6, /device:TPU:1, one launch (start us, length us, event | category | flops | bytes accessed | tf_op | source)
XLA Modules:
  0.0 30.9 jit_solution(9011587760167267083)
XLA Ops:
  0.6 29.6 %shard_map.140 = (bf16[16,128]{1,0:T(8,128)(2,1)S(1)}, f32[3,16]{1,0:T(4,128)S(1)}) custom-call(bf16[16,128]{1,0:T(8,128)(2,1)} %feat_hbm.1, bf16[3,16]{1,0:T(4,128)(2,1)} %place_hbm.1, s32[3,64]{1,0:T(4,128)} %table_hbm.1, bf16[128,128]{1,0:T(8,128)(2,1)} %w_tgt_hbm.1, bf16[128,128]{1,0:T(8,128)(2,1)} %w_src_hbm.1, f32[1,128]{1,0:T(1,128)} %bitcast.4, ...), custom_call_target="tpu_custom_call" | custom-call | tf_op jit(solution)/shard_map/pallas_call | solution.py:289
  30.3 0.6 %shard_map.141 = (bf16[16,128]{1,0:T(8,128)(2,1)}, f32[3,16]{1,0:T(4,128)}) custom-call(bf16[16,128]{1,0:T(8,128)(2,1)S(1)} %get-tuple-element.4.feat_in, f32[3,16]{1,0:T(4,128)S(1)} %get-tuple-element.5.place_in), custom_call_target="tpu_custom_call" | custom-call | tf_op jit(solution)/shard_map/pallas_call | solution.py:324

commit v7 on v6

--- a/solution.py
+++ b/solution.py
@@ -218,8 +218,8 @@
             from_spot = table[r, here * 2 + side] // 2
             picked_feat[side, r] = plane_feat[from_spot]
             picked_place[side, r] = plane_place[from_spot]
-    for to in range(16):
-        if to == 8:
+    for to in [k ^ 1 for k in range(16)]:
+        if to == 9:
 
             @pl.when(z_hi == 0)
             def _():

time: 31.1 us -> 30.8 us (level)
  no operation moved by 1% of the time
where the time goes in v7:
time: 30.8 us; the launch traced here: 30.6 us
  Pallas kernels  30 us (97%)
  between operations  0.64 us (2%)
    pallas_call x1, Pallas kernels, shards(): pl.pallas_call(layer, out_shape=(pltpu.VMEM((ROWS, 128), BF16), pltpu.VME...  29.4 us

profile of v7, /device:TPU:1, one launch (start us, length us, event | category | flops | bytes accessed | tf_op | source)
XLA Modules:
  0.0 30.6 jit_solution(11588431741102962369)
XLA Ops:
  0.6 29.4 %shard_map.140 = (bf16[16,128]{1,0:T(8,128)(2,1)S(1)}, f32[3,16]{1,0:T(4,128)S(1)}) custom-call(bf16[16,128]{1,0:T(8,128)(2,1)} %feat_hbm.1, bf16[3,16]{1,0:T(4,128)(2,1)} %place_hbm.1, s32[3,64]{1,0:T(4,128)} %table_hbm.1, bf16[128,128]{1,0:T(8,128)(2,1)} %w_tgt_hbm.1, bf16[128,128]{1,0:T(8,128)(2,1)} %w_src_hbm.1, f32[1,128]{1,0:T(1,128)} %bitcast.4, ...), custom_call_target="tpu_custom_call" | custom-call | tf_op jit(solution)/shard_map/pallas_call | solution.py:289
  30.0 0.6 %shard_map.141 = (bf16[16,128]{1,0:T(8,128)(2,1)}, f32[3,16]{1,0:T(4,128)}) custom-call(bf16[16,128]{1,0:T(8,128)(2,1)S(1)} %get-tuple-element.4.feat_in, f32[3,16]{1,0:T(4,128)S(1)} %get-tuple-element.5.place_in), custom_call_target="tpu_custom_call" | custom-call | tf_op jit(solution)/shard_map/pallas_call | solution.py:324
